TPU v7x, 32 devices: a whole 2x2x4 slice. The times are simulated.
32 devices in a mesh: space: 8 (over z, y), pairs: 4 (over x, core).
Axes of the slice: x: 2, y: 2, z: 4, core: 2. Of those that a mesh axis runs over, the one named last changes fastest.
Arguments:
- positions: float32 [2048, 3, 512], P(('space', 'pairs')), may hold values from -3 to 25.2, as said below
- forces: float32 [2048, 3, 512], P(('space', 'pairs')), may hold values from -6 to 6
- pair_cells: int32 [2, 1536], P(None, ('space', 'pairs')), may hold values from 0 to 2047, as said below
- pair_count: int32 [32], P(('space', 'pairs')), may hold values from 6 to 48, as said below
Outputs:
- velocity: float32 [2048, 3, 512], P(('space', 'pairs'))
Inputs may be any that keep to these rules, and one draw needn't show every extreme that they name: `pair_cells`: device g holds cells [g * 64, (g + 1) * 64). Row 0 of its slot columns names one of its own cells. Row 1 names a cell other than row 0's; over the 48 slots of one device it names cells of each of the 12 devices of the device's region and of the two regions beside it exactly 4 times, the first and the last region counting as beside each other. Slots at or past a device's count hold pairs too but are not in its list. `pair_count`: in every region one device holds 48 live slots. `positions`: the cells of region r have their first coordinates within 1.2 of [3 r, 3 r + 3); the other two coordinates lie within -3 to 5.
All inputs are finite; a program needn't handle non-finite values.
Results may differ from a plain program's by a relative error of at most 0.0003.
Values sent between devices are 32-bit elements; how exact they have to be, the bound alone decides.
No kernel may reach another device: no remote copies, remote signals or barrier semaphores. Data moves between devices by JAX's collectives and lax.ppermute only.
A program may use at most 128 MiB of HBM per device.

v0:
```python
import functools
import math

import jax
import jax.numpy as jnp
from jax import lax
from jax.experimental import pallas as pl
from jax.experimental.pallas import tpu as pltpu
from jax.sharding import PartitionSpec as P

stokes_coef = 1.0 / (8.0 * math.pi)
eps_sq = 0.01
slab_width = 3.0
across_middle = 1.0
LANES = 128
FEATURES = 16

f32 = jnp.float32
bf16 = jnp.bfloat16


def split(value, terms):
    parts = []
    for _ in range(terms - 1):
        part = value.astype(bf16).astype(f32)
        parts.append(part)
        value = value - part
    parts.append(value)
    return parts


def features(x, f):
    norm = jnp.sum(x * x, axis=0, keepdims=True)
    along = jnp.sum(x * f, axis=0, keepdims=True)
    rows = [f] + [x[k : k + 1] * f for k in range(3)] + [norm * f + x * along]
    rows.append(jnp.zeros_like(norm))
    stacked = jnp.concatenate(rows, axis=0)
    return jnp.concatenate([part.astype(bf16) for part in split(stacked, 3)], axis=0)


def combine(sums, y):
    force = sums[0:3]
    moment = [sums[3 + 3 * k : 6 + 3 * k] for k in range(3)]
    second = sums[12:15]
    norm = jnp.sum(y * y, axis=0, keepdims=True)
    trace = moment[0][0:1] + moment[1][1:2] + moment[2][2:3]
    along = jnp.sum(y * force, axis=0, keepdims=True) - trace
    turned = jnp.concatenate(
        [jnp.sum(y * moment[k], axis=0, keepdims=True) for k in range(3)], axis=0
    )
    mixed = y[0:1] * moment[0] + y[1:2] * moment[1] + y[2:3] * moment[2]
    velocity = (norm + 2.0 * eps_sq) * force + second - 2.0 * mixed + y * along - turned
    return velocity * stokes_coef


def gram_factors(x, y):
    one = jnp.ones((1, x.shape[1]), f32)
    none = jnp.zeros((3, x.shape[1]), f32)
    norm_x = jnp.sum(x * x, axis=0, keepdims=True)
    norm_y = jnp.sum(y * y, axis=0, keepdims=True) + eps_sq
    left = split(jnp.concatenate([x, norm_x, one, none], axis=0), 3)
    right = split(jnp.concatenate([-2.0 * y, one, norm_y, none], axis=0), 3)
    order = ((0, 0), (0, 1), (1, 0), (0, 2), (1, 1), (2, 0))
    return (
        jnp.concatenate([left[p] for p, _ in order], axis=0).astype(bf16),
        jnp.concatenate([right[q] for _, q in order], axis=0).astype(bf16),
    )


def dot(left, right, left_dim, right_dim):
    return lax.dot_general(
        left, right, (((left_dim,), (right_dim,)), ((), ())), preferred_element_type=f32
    )


def fold(high, low):
    return (
        high[0:FEATURES]
        + high[FEATURES : 2 * FEATURES]
        + high[2 * FEATURES :]
        + low[0:FEATURES]
        + low[FEATURES:]
    )


def weights(factors, half):
    left, right = factors
    dist_sq = dot(left[:, half], right, 0, 0)
    inverse = lax.rsqrt(dist_sq)
    cubed = inverse * inverse * inverse
    high = cubed.astype(bf16)
    return high, (cubed - high.astype(f32)).astype(bf16)


def pair_velocities(cells):
    two = 2 * FEATURES
    points = cells[0][0].shape[1]
    halves = [slice(0, points // 2), slice(points // 2, points)]
    factors = [gram_factors(xa, xb) for xa, _, xb, _ in cells]
    feats = [(features(xa, fa), features(xb, fb)) for xa, fa, xb, fb in cells]
    sums_a = [[] for _ in cells]
    sums_b = [[] for _ in cells]
    for half in halves:
        for i, (feat_a, feat_b) in enumerate(feats):
            high, low = weights(factors[i], half)
            part = feat_a[:, half]
            sums_b[i].append(fold(dot(part, high, 1, 0), dot(part[:two], low, 1, 0)))
            sums_a[i].append(fold(dot(feat_b, high, 1, 1), dot(feat_b[:two], low, 1, 1)))
    return [
        (
            combine(jnp.concatenate(sums_a[i], axis=1), xa),
            combine(sums_b[i][0] + sums_b[i][1], xb),
        )
        for i, (xa, _, xb, _) in enumerate(cells)
    ]


def row_base(cell, tiles):
    return cell // 8 * (8 * tiles) + lax.rem(cell, 8)


def away_of(kind, odd):
    return (0, 1 - 2 * odd, 2 * odd - 1)[kind]


def pack_kernel(sizes, cells, count, pos_hbm, frc_hbm, *refs):
    n_space, n_pairs, share, cell_dev, tiles = sizes
    outs, table = refs[:n_pairs], refs[n_pairs]
    slots, used, pos, frc, sems = refs[n_pairs + 1 :]
    fetches = [
        pltpu.make_async_copy(pos_hbm, pos, sems.at[0]),
        pltpu.make_async_copy(frc_hbm, frc, sems.at[1]),
    ]
    for fetch in fetches:
        fetch.start()
    n_slots = cells.shape[1]
    owner = cells[0, 0] // cell_dev
    here = owner // n_pairs
    here_turn = lax.rem(owner, n_pairs)
    table[n_slots] = here
    for bucket in range(3 * n_pairs):
        used[bucket] = 0
    for s in range(n_slots):
        owner = cells[1, s] // cell_dev
        there = owner // n_pairs
        turn = lax.rem(owner, n_pairs) ^ here_turn
        kind = jnp.where(there == here, 0, jnp.where(there // 2 == here // 2, 1, 2))
        bucket = kind * n_pairs + turn
        rank = used[bucket]
        used[bucket] = rank + 1
        slots[bucket * share + rank] = s
    for fetch in fetches:
        fetch.wait()
    lane = lax.broadcasted_iota(jnp.int32, (1, LANES), 1)
    plane = cell_dev * tiles
    for m in range(3 * n_pairs):
        kind, turn = m // n_pairs, m % n_pairs
        out = outs[turn]
        label = jnp.full((1, LANES), -1.0, f32)
        for k in range(share):
            s = slots[m * share + k]
            a = lax.rem(cells[0, s], cell_dev)
            live = s < count[0]
            b = jnp.where(live, lax.rem(cells[1, s], cell_dev), -1)
            table[m * share + k] = jnp.where(live, a, -1)
            label = jnp.where(lane == k, b.astype(f32), label)
            base = row_base(a, tiles)
            for c in range(6):
                source = pos if c < 3 else frc
                for t in range(tiles):
                    row = (k * tiles + t) * 6 + c
                    out[kind, row : row + 1, :] = source[
                        pl.ds(base + (c % 3 * plane + t * 8), 1), :
                    ]
        last = share * 6 * tiles
        out[kind, last : last + 1, :] = label


def pair_kernel(sizes, kind, n, started, table, *refs):
    n_space, n_pairs, share, cell_dev, tiles = sizes
    labels, messages = refs[:n], refs[n : 2 * n]
    pos, frc = refs[2 * n : 2 * n + 2]
    acc, reply, inbox, todo = refs[-4:]
    here = table[3 * n_pairs * share]
    away = jnp.int32(away_of(kind, lax.rem(here, 2)))
    there = lax.rem(here + away + n_space, n_space)
    half = 0.5 * slab_width * away.astype(f32)
    middle_a = slab_width * (there.astype(f32) + 0.5) - half
    middle_b = slab_width * (here.astype(f32) + 0.5) + half
    rows_in = share * 6 * tiles
    plane = cell_dev * tiles
    if started:
        acc[...] = refs[2 * n + 2][...]
    else:
        acc[...] = jnp.zeros_like(acc)
    number = jnp.int32(0)
    first = 0
    for label, message in zip(labels, messages):
        for block in range(message.shape[0]):
            inbox[first * rows_in : (first + 1) * rows_in, :] = message[block, 0:rows_in, :]
            for k in range(share):
                b = label[block, 0, k].astype(jnp.int32)
                todo[0, number] = first * share + k
                todo[1, number] = b
                number = number + jnp.where(b >= 0, 1, 0)
            first += 1

    axis = lax.broadcasted_iota(jnp.int32, (3, 1), 0)
    shift_a = jnp.where(axis == 0, middle_a, across_middle)
    shift_b = jnp.where(axis == 0, middle_b, across_middle)

    def load(i):
        base = todo[0, i] * (6 * tiles)
        data = jnp.concatenate(
            [inbox[pl.ds(base + 6 * t, 6), :] for t in range(tiles)], axis=1
        )
        start = row_base(todo[1, i], tiles)
        xb, fb = (
            jnp.concatenate(
                [
                    jnp.concatenate(
                        [ref[pl.ds(start + (c * plane + t * 8), 1), :] for t in range(tiles)],
                        axis=1,
                    )
                    for c in range(3)
                ],
                axis=0,
            )
            for ref in (pos, frc)
        )
        return data[0:3] - shift_a, data[3:6], xb - shift_b, fb

    def store(i, vel_a, vel_b):
        base = todo[0, i] * (3 * tiles)
        start = row_base(todo[1, i], tiles)
        for t in range(tiles):
            part = slice(t * LANES, (t + 1) * LANES)
            for c in range(3):
                acc[pl.ds(start + (c * plane + t * 8), 1), :] += vel_b[c : c + 1, part]
            reply[pl.ds(base + 3 * t, 3), :] = vel_a[:, part]

    def several(numbers):
        results = pair_velocities([load(i) for i in numbers])
        for i, result in zip(numbers, results):
            store(i, *result)

    def two(i, _):
        several([2 * i, 2 * i + 1])
        return 0

    lax.fori_loop(0, number // 2, two, 0)

    @pl.when(lax.rem(number, 2) == 1)
    def _():
        several([number - 1])


def add_kernel(sizes, table, acc, *refs):
    n_space, n_pairs, share, cell_dev, tiles = sizes
    replies, out = refs[:-1], refs[-1]
    plane = cell_dev * tiles
    out[...] = acc[...]
    for m in range(3 * n_pairs):
        kind, turn = m // n_pairs, m % n_pairs
        for k in range(share):
            a = table[m * share + k]
            live = a >= 0
            base = row_base(jnp.maximum(a, 0), tiles)
            for t in range(tiles):
                for c in range(3):
                    row = (k * tiles + t) * 3 + c
                    term = jnp.where(live, replies[turn][kind, row : row + 1, :], 0.0)
                    out[pl.ds(base + (c * plane + t * 8), 1), :] += term


def flat_rows(cells):
    count, _, points = cells.shape
    value = jnp.transpose(cells, (1, 0, 2)).reshape(3, count // 8, 8, points // LANES, LANES)
    return jnp.transpose(value, (0, 1, 3, 2, 4)).reshape(-1, LANES)


def cell_rows(rows, count, points):
    value = rows.reshape(3, count // 8, points // LANES, 8, LANES)
    value = jnp.transpose(value, (0, 1, 3, 2, 4)).reshape(3, count, points)
    return jnp.transpose(value, (1, 0, 2))


def body(positions, forces, pair_cells, pair_count):
    n_space = lax.axis_size("space")
    n_pairs = lax.axis_size("pairs")
    cell_dev, _, points = positions.shape
    n_slots = pair_cells.shape[1]
    share = n_slots // (3 * n_pairs)
    tiles = points // LANES
    sizes = (n_space, n_pairs, share, cell_dev, tiles)
    rows_in = share * 6 * tiles
    rows_out = share * 3 * tiles
    pos = flat_rows(positions)
    frc = flat_rows(forces)
    vmem = pl.BlockSpec(memory_space=pltpu.VMEM)
    smem = pl.BlockSpec(memory_space=pltpu.SMEM)
    hbm = pl.BlockSpec(memory_space=pltpu.HBM)
    message = jax.ShapeDtypeStruct((3, rows_in + 8, LANES), f32)
    total = jax.ShapeDtypeStruct((3 * cell_dev * tiles, LANES), f32)

    def across(value, turn):
        return lax.ppermute(value, "pairs", [(j, j ^ turn) for j in range(n_pairs)])

    def beyond(value, kind):
        moves = [(i, (i + away_of(kind, i % 2)) % n_space) for i in range(n_space)]
        return lax.ppermute(value, "space", moves)

    packed = pl.pallas_call(
        functools.partial(pack_kernel, sizes),
        out_shape=[message] * n_pairs + [jax.ShapeDtypeStruct((n_slots + 1,), jnp.int32)],
        in_specs=[smem, smem, hbm, hbm],
        out_specs=[vmem] * n_pairs + [smem],
        scratch_shapes=[
            pltpu.SMEM((n_slots,), jnp.int32),
            pltpu.SMEM((3 * n_pairs,), jnp.int32),
            pltpu.VMEM(total.shape, f32),
            pltpu.VMEM(total.shape, f32),
            pltpu.SemaphoreType.DMA((2,)),
        ],
        compiler_params=pltpu.CompilerParams(vmem_limit_bytes=60 * 1024 * 1024),
        name="pack",
    )(pair_cells, pair_count, pos, frc)
    sent, table = packed[:n_pairs], packed[n_pairs]
    got = [sent[0]] + [across(sent[turn], turn) for turn in range(1, n_pairs)]

    def pairs(kind, arrived, before, own=False):
        n = len(arrived)
        blocks = 1 if kind == 0 else n_pairs
        part = kind if kind == 0 else 0
        label = pl.BlockSpec(
            (blocks, 8, LANES), lambda i: (part, rows_in // 8, 0), memory_space=pltpu.SMEM
        )
        data = pl.BlockSpec((blocks, rows_in + 8, LANES), lambda i: (part, 0, 0))
        work = 1 if own else 4
        return pl.pallas_call(
            functools.partial(pair_kernel, sizes, kind, n, len(before) == 1),
            out_shape=[total, jax.ShapeDtypeStruct((n * blocks * rows_out, LANES), f32)],
            grid=(1,),
            in_specs=[smem] + [label] * n + [data] * n + [vmem] * (2 + len(before)),
            out_specs=[vmem] * 2,
            scratch_shapes=[
                pltpu.VMEM((n * blocks * rows_in, LANES), f32),
                pltpu.SMEM((2, n * blocks * share + 1), jnp.int32),
            ],
            compiler_params=pltpu.CompilerParams(vmem_limit_bytes=48 * 1024 * 1024),
            cost_estimate=pl.CostEstimate(
                flops=work * 1_000_000_000, bytes_accessed=2_000_000, transcendentals=2_000_000
            ),
            name="pairs",
        )(table, *arrived, *arrived, pos, frc, *before)

    acc, reply_own = pairs(0, got[:1], [], True)
    out_1 = beyond(jnp.stack([value[1] for value in got]), 1)
    out_2 = beyond(jnp.stack([value[2] for value in got]), 2)
    acc, reply_0 = pairs(0, got[1:], [acc])
    acc, reply_1 = pairs(1, [out_1], [acc])
    back_1 = beyond(reply_1, 1)
    acc, reply_2 = pairs(2, [out_2], [acc])
    back_2 = beyond(reply_2, 2)
    back_0 = jnp.concatenate([reply_own, reply_0], axis=0)
    shape = (n_pairs, rows_out, LANES)
    back_0, back_1, back_2 = (value.reshape(shape) for value in (back_0, back_1, back_2))
    back = []
    for turn in range(n_pairs):
        value = jnp.stack([back_0[turn], back_1[turn], back_2[turn]])
        back.append(across(value, turn) if turn else value)
    velocity = pl.pallas_call(
        functools.partial(add_kernel, sizes),
        out_shape=total,
        in_specs=[smem] + [vmem] * (1 + n_pairs),
        out_specs=vmem,
        compiler_params=pltpu.CompilerParams(vmem_limit_bytes=48 * 1024 * 1024),
        name="add",
    )(table, acc, *back)
    return cell_rows(velocity, cell_dev, points)


def solution(mesh):
    placed = (
        P(("space", "pairs"), None, None),
        P(("space", "pairs"), None, None),
        P(None, ("space", "pairs")),
        P(("space", "pairs")),
    )
    return jax.shard_map(
        body,
        mesh=mesh,
        in_specs=placed,
        out_specs=P(("space", "pairs"), None, None),
        check_vma=False,
    )
```

profile of v0, /device:TPU:0, one launch (start us, length us, event | category | flops | bytes accessed | tf_op | source)
XLA Modules:
  0.0 63.7 jit_solution(11732350503509542809)
XLA Ops:
  0.7 3.7 %pack.1 = (f32[3,104,128]{2,1,0:T(8,128)}, f32[3,104,128]{2,1,0:T(8,128)}, f32[3,104,128]{2,1,0:T(8,128)}, f32[3,104,128]{2,1,0:T(8,128)}, s32[49]{0:T(128)}) custom-call(s32[2,48]{1,0:T(2,128)} %cells.1, s32[1]{0:T(128)S(6)} %copy.5.count, f32[768,128]{1,0:T(8,128)} %bitcast.44, f32[768,128]{1,0:T(8,128)} %bitcast.49), custom_call_target="tpu_custom_call" | custom-call | tf_op jit(solution)/shard_map/pack/pallas_call | solution.py:313
  4.4 0.0 copy-start.2
  4.4 0.5 collective-permute-start
  4.9 2.6 %collective-permute-start.1 = (f32[3,104,128]{2,1,0:T(8,128)}, f32[3,104,128]{2,1,0:T(8,128)S(1)}, u32[]{:S(2)}, u32[]{:S(2)}) collective-permute-start(f32[3,104,128]{2,1,0:T(8,128)} %get-tuple-element.21), channel_id=1, source_target_pairs={{0,2},{1,3},{2,0},{3,1},{4,6},{5,7},{6,4},{7,5},{8,10},{9,11},{10,... | collective-permute-start | bytes 479240 | tf_op jit(solution)/shard_map/ppermute | solution.py:307
  7.4 0.1 collective-permute-start.2
  7.5 0.8 %fusion = (f32[1,104,128]{2,1,0:T(8,128)S(1)}, f32[1,104,128]{2,1,0:T(8,128)S(1)}) fusion(f32[3,104,128]{2,1,0:T(8,128)} %get-tuple-element.19.refs_0_.refs_1_), kind=kLoop, calls=%fused_computation.17 | loop fusion | bytes 212992 | tf_op jit(solution)/shard_map/slice | solution.py:358
  8.4 0.0 copy-done
  8.4 0.0 copy-done.1
  8.4 0.0 copy-done.2
  8.4 0.6 copy-done.3
  9.0 1.8 %pairs.4 = (f32[768,128]{1,0:T(8,128)S(1)}, f32[48,128]{1,0:T(8,128)S(1)}) custom-call(s32[49]{0:T(128)S(1)} %copy-done.3, f32[3,104,128]{2,1,0:T(8,128)S(1)} %copy-done.2, f32[3,104,128]{2,1,0:T(8,128)S(1)} %copy-done.2, f32[768,128]{1,0:T(8,128)S(1)} %bitcast.45, f32[768,128]{1,0:T(8,128)S(1)} %bitcast.50), custom_call_target="tpu_custom_call" | custom-call | flops 1000000000 | bytes 2000000 | tf_op jit(solution)/shard_map/pairs/pallas_call | solution.py:340
  10.8 0.0 collective-permute-done.refs_0_.refs_3_
  10.8 1.8 %collective-permute-done.1.refs_1_.refs_4_ = f32[3,104,128]{2,1,0:T(8,128)S(1)} collective-permute-done((f32[3,104,128]{2,1,0:T(8,128)}, f32[3,104,128]{2,1,0:T(8,128)S(1)}, u32[]{:S(2)}, u32[]{:S(2)}) %collective-permute-start.1) | collective-permute-done | bytes 159776 | tf_op jit(solution)/shard_map/ppermute | solution.py:307
  12.6 2.9 %collective-permute-done.2.refs_2_.refs_5_ = f32[3,104,128]{2,1,0:T(8,128)S(1)} collective-permute-done((f32[3,104,128]{2,1,0:T(8,128)}, f32[3,104,128]{2,1,0:T(8,128)S(1)}, u32[]{:S(2)}, u32[]{:S(2)}) %collective-permute-start.2) | collective-permute-done | bytes 159776 | tf_op jit(solution)/shard_map/ppermute | solution.py:307
  15.6 1.7 %collective-permute-start.4 = (f32[4,104,128]{2,1,0:T(8,128)S(1)}, f32[4,104,128]{2,1,0:T(8,128)S(1)}, u32[]{:S(2)}, u32[]{:S(2)}) collective-permute-start(f32[4,104,128]{2,1,0:T(8,128)S(1)} %pad_maximum_fusion.1), channel_id=1, source_target_pairs={{0,4},{4,0},{8,12},{12,8},{16,20},{20,16},{24,28},{28,24},{1,5},{5... | collective-permute-start | bytes 638984 | tf_op jit(solution)/shard_map/ppermute | solution.py:311
  17.2 3.6 %collective-permute-start.3 = (f32[4,104,128]{2,1,0:T(8,128)S(1)}, f32[4,104,128]{2,1,0:T(8,128)S(1)}, u32[]{:S(2)}, u32[]{:S(2)}) collective-permute-start(f32[4,104,128]{2,1,0:T(8,128)S(1)} %pad_maximum_fusion), channel_id=1, source_target_pairs={{0,28},{4,8},{8,4},{12,16},{16,12},{20,24},{24,20},{28,0},{1,29},{... | collective-permute-start | bytes 638984 | tf_op jit(solution)/shard_map/ppermute | solution.py:311
  20.8 4.7 %pairs.5 = (f32[768,128]{1,0:T(8,128)S(1)}, f32[144,128]{1,0:T(8,128)S(1)}) custom-call(s32[49]{0:T(128)S(1)} %copy-done.3, f32[3,104,128]{2,1,0:T(8,128)S(1)} %collective-permute-done.refs_0_.refs_3_, f32[3,104,128]{2,1,0:T(8,128)S(1)} %collective-permute-done.1.refs_1_.refs_4_, f32[3,104,128]{2,1,0:T(8,128)S(1)} %collective-permute-done.2.refs_2_.refs_5_, ...), custom_call_target="tpu_custom_call" | custom-call | flops 4000000000 | bytes 2000000 | tf_op jit(solution)/shard_map/pairs/pallas_call | solution.py:340
  25.5 2.0 %collective-permute-done.4.refs_0_.refs_1_ = f32[4,104,128]{2,1,0:T(8,128)S(1)} collective-permute-done((f32[4,104,128]{2,1,0:T(8,128)S(1)}, f32[4,104,128]{2,1,0:T(8,128)S(1)}, u32[]{:S(2)}, u32[]{:S(2)}) %collective-permute-start.4) | collective-permute-done | bytes 213024 | tf_op jit(solution)/shard_map/ppermute | solution.py:311
  27.5 6.7 %pairs.6 = (f32[768,128]{1,0:T(8,128)S(1)}, f32[192,128]{1,0:T(8,128)S(1)}) custom-call(s32[49]{0:T(128)S(1)} %copy-done.3, f32[4,104,128]{2,1,0:T(8,128)S(1)} %collective-permute-done.4.refs_0_.refs_1_, f32[4,104,128]{2,1,0:T(8,128)S(1)} %collective-permute-done.4.refs_0_.refs_1_, f32[768,128]{1,0:T(8,128)S(1)} %bitcast.47, f32[768,128]{1,0:T(8,128)S(1)} %bitcast.52, ...), custom_call_target="tpu_custom_call" | custom-call | flops 4000000000 | bytes 2000000 | tf_op jit(solution)/shard_map/pairs/pallas_call | solution.py:340
  34.1 0.0 collective-permute-done.3.refs_0_.refs_1_
  34.2 7.8 %pairs.7 = (f32[768,128]{1,0:T(8,128)S(1)}, f32[192,128]{1,0:T(8,128)S(1)}) custom-call(s32[49]{0:T(128)S(1)} %copy-done.3, f32[4,104,128]{2,1,0:T(8,128)S(1)} %collective-permute-done.3.refs_0_.refs_1_, f32[4,104,128]{2,1,0:T(8,128)S(1)} %collective-permute-done.3.refs_0_.refs_1_, f32[768,128]{1,0:T(8,128)S(1)} %bitcast.48, f32[768,128]{1,0:T(8,128)S(1)} %bitcast.53, ...), custom_call_target="tpu_custom_call" | custom-call | flops 4000000000 | bytes 2000000 | tf_op jit(solution)/shard_map/pairs/pallas_call | solution.py:340
  42.0 7.5 %collective-permute-start.6 = (f32[192,128]{1,0:T(8,128)S(1)}, f32[192,128]{1,0:T(8,128)S(1)}, u32[]{:S(2)}, u32[]{:S(2)}) collective-permute-start(f32[192,128]{1,0:T(8,128)S(1)} %get-tuple-element.29), channel_id=1, source_target_pairs={{0,28},{4,8},{8,4},{12,16},{16,12},{20,24},{24,20},{28,0},{1,29},{... | collective-permute-start | bytes 294920 | tf_op jit(solution)/shard_map/ppermute | solution.py:311
  49.5 2.8 %collective-permute-start.5 = (f32[192,128]{1,0:T(8,128)S(1)}, f32[192,128]{1,0:T(8,128)S(1)}, u32[]{:S(2)}, u32[]{:S(2)}) collective-permute-start(f32[192,128]{1,0:T(8,128)S(1)} %get-tuple-element.28), channel_id=1, source_target_pairs={{0,4},{4,0},{8,12},{12,8},{16,20},{20,16},{24,28},{28,24},{1,5},{5... | collective-permute-start | bytes 294920 | tf_op jit(solution)/shard_map/ppermute | solution.py:311
  52.3 0.0 collective-permute-done.6
  52.3 3.4 %collective-permute-done.5 = f32[192,128]{1,0:T(8,128)S(1)} collective-permute-done((f32[192,128]{1,0:T(8,128)S(1)}, f32[192,128]{1,0:T(8,128)S(1)}, u32[]{:S(2)}, u32[]{:S(2)}) %collective-permute-start.5) | collective-permute-done | bytes 98336 | tf_op jit(solution)/shard_map/ppermute | solution.py:311
  55.8 0.1 collective-permute-start.9
  55.9 1.5 %collective-permute-start.8 = (f32[3,48,128]{2,1,0:T(8,128)S(1)}, f32[3,48,128]{2,1,0:T(8,128)S(1)}, u32[]{:S(2)}, u32[]{:S(2)}) collective-permute-start(f32[3,48,128]{2,1,0:T(8,128)S(1)} %pad_maximum_fusion.4), channel_id=1, source_target_pairs={{0,2},{1,3},{2,0},{3,1},{4,6},{5,7},{6,4},{7,5},{8,10},{9,11},{10,... | collective-permute-start | bytes 221192 | tf_op jit(solution)/shard_map/ppermute | solution.py:307
  57.3 0.4 collective-permute-start.7
  57.7 2.6 %collective-permute-done.9.refs_3_ = f32[3,48,128]{2,1,0:T(8,128)S(1)} collective-permute-done((f32[3,48,128]{2,1,0:T(8,128)S(1)}, f32[3,48,128]{2,1,0:T(8,128)S(1)}, u32[]{:S(2)}, u32[]{:S(2)}) %collective-permute-start.9) | collective-permute-done | bytes 73760 | tf_op jit(solution)/shard_map/ppermute | solution.py:307
  60.3 1.6 %collective-permute-done.8.refs_2_ = f32[3,48,128]{2,1,0:T(8,128)S(1)} collective-permute-done((f32[3,48,128]{2,1,0:T(8,128)S(1)}, f32[3,48,128]{2,1,0:T(8,128)S(1)}, u32[]{:S(2)}, u32[]{:S(2)}) %collective-permute-start.8) | collective-permute-done | bytes 73760 | tf_op jit(solution)/shard_map/ppermute | solution.py:307
  62.0 0.0 collective-permute-done.7.refs_1_
  62.0 1.7 %add.1 = f32[768,128]{1,0:T(8,128)} custom-call(s32[49]{0:T(128)S(1)} %copy-done.3, f32[768,128]{1,0:T(8,128)S(1)} %get-tuple-element.26.acc, f32[3,48,128]{2,1,0:T(8,128)S(1)} %pad_maximum_fusion.2.refs_0_, f32[3,48,128]{2,1,0:T(8,128)S(1)} %collective-permute-done.7.refs_1_, f32[3,48,128]{2,1,0:T(8,128)S(1)} %collective-permute-done.8.refs_2_, ...), custom_call_target="tpu_custom_call" | custom-call | tf_op jit(solution)/shard_map/add/pallas_call | solution.py:372
  (15 shorter events, 0.1 us)
Async XLA Ops:
  0.7 7.7 %copy-start = (f32[64,3,512]{2,0,1:T(8,128)S(1)}, f32[64,3,512]{2,0,1:T(8,128)}, u32[]{:S(2)}) copy-start(f32[64,3,512]{2,0,1:T(8,128)} %param.4) | copy-start | bytes 1179652
  0.7 7.7 %copy-start.1 = (f32[64,3,512]{2,0,1:T(8,128)S(1)}, f32[64,3,512]{2,0,1:T(8,128)}, u32[]{:S(2)}) copy-start(f32[64,3,512]{2,0,1:T(8,128)} %param.5) | copy-start | bytes 1179652
  4.4 4.0 %copy-start.2 = (f32[3,104,128]{2,1,0:T(8,128)S(1)}, f32[3,104,128]{2,1,0:T(8,128)}, u32[]{:S(2)}) copy-start(f32[3,104,128]{2,1,0:T(8,128)} %get-tuple-element.19.refs_0_.refs_1_) | copy-start | bytes 479236
  4.4 6.4 %collective-permute-start = (f32[3,104,128]{2,1,0:T(8,128)}, f32[3,104,128]{2,1,0:T(8,128)S(1)}, u32[]{:S(2)}, u32[]{:S(2)}) collective-permute-start(f32[3,104,128]{2,1,0:T(8,128)} %get-tuple-element.20), channel_id=1, source_target_pairs={{0,1},{1,0},{2,3},{3,2},{4,5},{5,4},{6,7},{7,6},{8,9},{9,8},{10,11... | collective-permute-start | bytes 479240 | tf_op jit(solution)/shard_map/ppermute | solution.py:307
  4.9 7.7 %collective-permute-start.1 = (f32[3,104,128]{2,1,0:T(8,128)}, f32[3,104,128]{2,1,0:T(8,128)S(1)}, u32[]{:S(2)}, u32[]{:S(2)}) collective-permute-start(f32[3,104,128]{2,1,0:T(8,128)} %get-tuple-element.21), channel_id=1, source_target_pairs={{0,2},{1,3},{2,0},{3,1},{4,6},{5,7},{6,4},{7,5},{8,10},{9,11},{10,... | collective-permute-start | bytes 479240 | tf_op jit(solution)/shard_map/ppermute | solution.py:307
  7.4 8.1 %collective-permute-start.2 = (f32[3,104,128]{2,1,0:T(8,128)}, f32[3,104,128]{2,1,0:T(8,128)S(1)}, u32[]{:S(2)}, u32[]{:S(2)}) collective-permute-start(f32[3,104,128]{2,1,0:T(8,128)} %get-tuple-element.22), channel_id=1, source_target_pairs={{0,3},{1,2},{2,1},{3,0},{4,7},{5,6},{6,5},{7,4},{8,11},{9,10},{10,... | collective-permute-start | bytes 479240 | tf_op jit(solution)/shard_map/ppermute | solution.py:307
  8.4 0.6 copy-start.3
  15.6 11.9 %collective-permute-start.4 = (f32[4,104,128]{2,1,0:T(8,128)S(1)}, f32[4,104,128]{2,1,0:T(8,128)S(1)}, u32[]{:S(2)}, u32[]{:S(2)}) collective-permute-start(f32[4,104,128]{2,1,0:T(8,128)S(1)} %pad_maximum_fusion.1), channel_id=1, source_target_pairs={{0,4},{4,0},{8,12},{12,8},{16,20},{20,16},{24,28},{28,24},{1,5},{5... | collective-permute-start | bytes 638984 | tf_op jit(solution)/shard_map/ppermute | solution.py:311
  17.2 16.9 %collective-permute-start.3 = (f32[4,104,128]{2,1,0:T(8,128)S(1)}, f32[4,104,128]{2,1,0:T(8,128)S(1)}, u32[]{:S(2)}, u32[]{:S(2)}) collective-permute-start(f32[4,104,128]{2,1,0:T(8,128)S(1)} %pad_maximum_fusion), channel_id=1, source_target_pairs={{0,28},{4,8},{8,4},{12,16},{16,12},{20,24},{24,20},{28,0},{1,29},{... | collective-permute-start | bytes 638984 | tf_op jit(solution)/shard_map/ppermute | solution.py:311
  42.0 10.3 %collective-permute-start.6 = (f32[192,128]{1,0:T(8,128)S(1)}, f32[192,128]{1,0:T(8,128)S(1)}, u32[]{:S(2)}, u32[]{:S(2)}) collective-permute-start(f32[192,128]{1,0:T(8,128)S(1)} %get-tuple-element.29), channel_id=1, source_target_pairs={{0,28},{4,8},{8,4},{12,16},{16,12},{20,24},{24,20},{28,0},{1,29},{... | collective-permute-start | bytes 294920 | tf_op jit(solution)/shard_map/ppermute | solution.py:311
  49.5 6.2 %collective-permute-start.5 = (f32[192,128]{1,0:T(8,128)S(1)}, f32[192,128]{1,0:T(8,128)S(1)}, u32[]{:S(2)}, u32[]{:S(2)}) collective-permute-start(f32[192,128]{1,0:T(8,128)S(1)} %get-tuple-element.28), channel_id=1, source_target_pairs={{0,4},{4,0},{8,12},{12,8},{16,20},{20,16},{24,28},{28,24},{1,5},{5... | collective-permute-start | bytes 294920 | tf_op jit(solution)/shard_map/ppermute | solution.py:311
  55.8 4.6 %collective-permute-start.9 = (f32[3,48,128]{2,1,0:T(8,128)S(1)}, f32[3,48,128]{2,1,0:T(8,128)S(1)}, u32[]{:S(2)}, u32[]{:S(2)}) collective-permute-start(f32[3,48,128]{2,1,0:T(8,128)S(1)} %pad_maximum_fusion.5), channel_id=1, source_target_pairs={{0,3},{1,2},{2,1},{3,0},{4,7},{5,6},{6,5},{7,4},{8,11},{9,10},{10,... | collective-permute-start | bytes 221192 | tf_op jit(solution)/shard_map/ppermute | solution.py:307
  55.9 6.1 %collective-permute-start.8 = (f32[3,48,128]{2,1,0:T(8,128)S(1)}, f32[3,48,128]{2,1,0:T(8,128)S(1)}, u32[]{:S(2)}, u32[]{:S(2)}) collective-permute-start(f32[3,48,128]{2,1,0:T(8,128)S(1)} %pad_maximum_fusion.4), channel_id=1, source_target_pairs={{0,2},{1,3},{2,0},{3,1},{4,6},{5,7},{6,4},{7,5},{8,10},{9,11},{10,... | collective-permute-start | bytes 221192 | tf_op jit(solution)/shard_map/ppermute | solution.py:307
  57.3 4.6 %collective-permute-start.7 = (f32[3,48,128]{2,1,0:T(8,128)S(1)}, f32[3,48,128]{2,1,0:T(8,128)S(1)}, u32[]{:S(2)}, u32[]{:S(2)}) collective-permute-start(f32[3,48,128]{2,1,0:T(8,128)S(1)} %pad_maximum_fusion.3), channel_id=1, source_target_pairs={{0,1},{1,0},{2,3},{3,2},{4,5},{5,4},{6,7},{7,6},{8,9},{9,8},{10,11... | collective-permute-start | bytes 221192 | tf_op jit(solution)/shard_map/ppermute | solution.py:307
where the time goes:
time: 63 us; the launch traced here: 63.7 us
  Pallas kernels  26.4 us (42%)
  starting transfers between devices  20.6 us (33%)
  waiting for transfers between devices  14.3 us (23%)
  local copies, waits for them, and re-layouts  1.5 us (2%)
  between operations  0.81 us (1%)
    pallas_call x4, Pallas kernels, pairs(): pl.pallas_call(functools.partial(pair_kernel, sizes, kind, n, len(before)...  21 us
    ppermute x4, starting transfers between devices, beyond(): return lax.ppermute(value, 'space', moves)  15.6 us
    ppermute x6, waiting for transfers between devices, across(): return lax.ppermute(value, 'pairs', [(j, j ^ turn) for j in range(n_pairs)])  8.95 us
    ppermute x4, waiting for transfers between devices, beyond(): return lax.ppermute(value, 'space', moves)  5.37 us
    ppermute x6, starting transfers between devices, across(): return lax.ppermute(value, 'pairs', [(j, j ^ turn) for j in range(n_pairs)])  5.06 us
    pallas_call x1, Pallas kernels, body(): pl.pallas_call(functools.partial(pack_kernel, sizes), out_shape=[message]...  3.67 us
    pallas_call x1, Pallas kernels, body(): pl.pallas_call(functools.partial(add_kernel, sizes), out_shape=total, in_...  1.72 us
  transfers between devices with their start and end apart: 10, of which 6 were waited for; matrix products, arithmetic and copies ran while one was open for 1% of the time, Pallas kernels for 21%

commit v1 on v0

--- a/solution.py
+++ b/solution.py
@@ -83,9 +83,8 @@
     )
 
 
-def weights(factors, half):
-    left, right = factors
-    dist_sq = dot(left[:, half], right, 0, 0)
+def weights(factors):
+    dist_sq = dot(*factors, 0, 0)
     inverse = lax.rsqrt(dist_sq)
     cubed = inverse * inverse * inverse
     high = cubed.astype(bf16)
@@ -94,24 +93,17 @@
 
 def pair_velocities(cells):
     two = 2 * FEATURES
-    points = cells[0][0].shape[1]
-    halves = [slice(0, points // 2), slice(points // 2, points)]
     factors = [gram_factors(xa, xb) for xa, _, xb, _ in cells]
     feats = [(features(xa, fa), features(xb, fb)) for xa, fa, xb, fb in cells]
-    sums_a = [[] for _ in cells]
-    sums_b = [[] for _ in cells]
-    for half in halves:
-        for i, (feat_a, feat_b) in enumerate(feats):
-            high, low = weights(factors[i], half)
-            part = feat_a[:, half]
-            sums_b[i].append(fold(dot(part, high, 1, 0), dot(part[:two], low, 1, 0)))
-            sums_a[i].append(fold(dot(feat_b, high, 1, 1), dot(feat_b[:two], low, 1, 1)))
+    sums = []
+    for factor, (feat_a, feat_b) in zip(factors, feats):
+        high, low = weights(factor)
+        sums_b = fold(dot(feat_a, high, 1, 0), dot(feat_a[:two], low, 1, 0))
+        sums_a = fold(dot(feat_b, high, 1, 1), dot(feat_b[:two], low, 1, 1))
+        sums.append((sums_a, sums_b))
     return [
-        (
-            combine(jnp.concatenate(sums_a[i], axis=1), xa),
-            combine(sums_b[i][0] + sums_b[i][1], xb),
-        )
-        for i, (xa, _, xb, _) in enumerate(cells)
+        (combine(sums_a, xa), combine(sums_b, xb))
+        for (sums_a, sums_b), (xa, _, xb, _) in zip(sums, cells)
     ]
 
 
@@ -176,17 +168,16 @@
         out[kind, last : last + 1, :] = label
 
 
-def pair_kernel(sizes, kind, n, started, table, *refs):
+def pair_kernel(sizes, kinds, started, table, *refs):
     n_space, n_pairs, share, cell_dev, tiles = sizes
+    n = len(kinds)
     labels, messages = refs[:n], refs[n : 2 * n]
     pos, frc = refs[2 * n : 2 * n + 2]
-    acc, reply, inbox, todo = refs[-4:]
+    outs = refs[2 * n + 2 + started :]
+    (acc, reply), (inbox, todo, middles) = outs[:2], outs[-3:]
+    if not started:
+        outs[2][...] = jnp.zeros_like(outs[2])
     here = table[3 * n_pairs * share]
-    away = jnp.int32(away_of(kind, lax.rem(here, 2)))
-    there = lax.rem(here + away + n_space, n_space)
-    half = 0.5 * slab_width * away.astype(f32)
-    middle_a = slab_width * (there.astype(f32) + 0.5) - half
-    middle_b = slab_width * (here.astype(f32) + 0.5) + half
     rows_in = share * 6 * tiles
     plane = cell_dev * tiles
     if started:
@@ -195,19 +186,24 @@
         acc[...] = jnp.zeros_like(acc)
     number = jnp.int32(0)
     first = 0
-    for label, message in zip(labels, messages):
+    for kind, label, message in zip(kinds, labels, messages):
+        away = jnp.int32(away_of(kind, lax.rem(here, 2)))
+        there = lax.rem(here + away + n_space, n_space)
+        half = 0.5 * slab_width * away.astype(f32)
+        middle_a = slab_width * (there.astype(f32) + 0.5) - half
+        middle_b = slab_width * (here.astype(f32) + 0.5) + half
         for block in range(message.shape[0]):
             inbox[first * rows_in : (first + 1) * rows_in, :] = message[block, 0:rows_in, :]
             for k in range(share):
                 b = label[block, 0, k].astype(jnp.int32)
                 todo[0, number] = first * share + k
                 todo[1, number] = b
+                middles[0, number] = middle_a
+                middles[1, number] = middle_b
                 number = number + jnp.where(b >= 0, 1, 0)
             first += 1
 
     axis = lax.broadcasted_iota(jnp.int32, (3, 1), 0)
-    shift_a = jnp.where(axis == 0, middle_a, across_middle)
-    shift_b = jnp.where(axis == 0, middle_b, across_middle)
 
     def load(i):
         base = todo[0, i] * (6 * tiles)
@@ -228,7 +224,9 @@
             )
             for ref in (pos, frc)
         )
-        return data[0:3] - shift_a, data[3:6], xb - shift_b, fb
+        xa = data[0:3] - jnp.where(axis == 0, middles[0, i], across_middle)
+        xb = xb - jnp.where(axis == 0, middles[1, i], across_middle)
+        return xa, data[3:6], xb, fb
 
     def store(i, vel_a, vel_b):
         base = todo[0, i] * (3 * tiles)
@@ -328,43 +326,64 @@
     sent, table = packed[:n_pairs], packed[n_pairs]
     got = [sent[0]] + [across(sent[turn], turn) for turn in range(1, n_pairs)]
 
-    def pairs(kind, arrived, before, own=False):
-        n = len(arrived)
-        blocks = 1 if kind == 0 else n_pairs
-        part = kind if kind == 0 else 0
-        label = pl.BlockSpec(
-            (blocks, 8, LANES), lambda i: (part, rows_in // 8, 0), memory_space=pltpu.SMEM
-        )
-        data = pl.BlockSpec((blocks, rows_in + 8, LANES), lambda i: (part, 0, 0))
-        work = 1 if own else 4
+    def pairs(arrived, before):
+        kinds, values, labels, data = [], [], [], []
+        for kind, value, whole in arrived:
+            blocks = value.shape[0] if whole else 1
+            part = 0 if whole else kind
+            kinds += [kind]
+            values += [value]
+            labels.append(
+                pl.BlockSpec(
+                    (blocks, 8, LANES),
+                    functools.partial(lambda part, i: (part, rows_in // 8, 0), part),
+                    memory_space=pltpu.SMEM,
+                )
+            )
+            data.append(
+                pl.BlockSpec(
+                    (blocks, rows_in + 8, LANES),
+                    functools.partial(lambda part, i: (part, 0, 0), part),
+                )
+            )
+        total_blocks = sum(spec.block_shape[0] for spec in data)
         return pl.pallas_call(
-            functools.partial(pair_kernel, sizes, kind, n, len(before) == 1),
-            out_shape=[total, jax.ShapeDtypeStruct((n * blocks * rows_out, LANES), f32)],
+            functools.partial(pair_kernel, sizes, kinds, len(before) == 1),
+            out_shape=[total, jax.ShapeDtypeStruct((total_blocks * rows_out, LANES), f32)]
+            + [jax.ShapeDtypeStruct((1, LANES), f32)] * (not before),
             grid=(1,),
-            in_specs=[smem] + [label] * n + [data] * n + [vmem] * (2 + len(before)),
-            out_specs=[vmem] * 2,
+            in_specs=[smem] + labels + data + [vmem] * (2 + len(before)),
+            out_specs=[vmem] * (2 + (not before)),
             scratch_shapes=[
-                pltpu.VMEM((n * blocks * rows_in, LANES), f32),
-                pltpu.SMEM((2, n * blocks * share + 1), jnp.int32),
+                pltpu.VMEM((total_blocks * rows_in, LANES), f32),
+                pltpu.SMEM((2, total_blocks * share + 1), jnp.int32),
+                pltpu.SMEM((2, total_blocks * share + 1), f32),
             ],
             compiler_params=pltpu.CompilerParams(vmem_limit_bytes=48 * 1024 * 1024),
             cost_estimate=pl.CostEstimate(
-                flops=work * 1_000_000_000, bytes_accessed=2_000_000, transcendentals=2_000_000
+                flops=total_blocks * 1_000_000_000, bytes_accessed=2_000_000, transcendentals=2_000_000
             ),
             name="pairs",
-        )(table, *arrived, *arrived, pos, frc, *before)
-
-    acc, reply_own = pairs(0, got[:1], [], True)
-    out_1 = beyond(jnp.stack([value[1] for value in got]), 1)
-    out_2 = beyond(jnp.stack([value[2] for value in got]), 2)
-    acc, reply_0 = pairs(0, got[1:], [acc])
-    acc, reply_1 = pairs(1, [out_1], [acc])
-    back_1 = beyond(reply_1, 1)
-    acc, reply_2 = pairs(2, [out_2], [acc])
-    back_2 = beyond(reply_2, 2)
-    back_0 = jnp.concatenate([reply_own, reply_0], axis=0)
-    shape = (n_pairs, rows_out, LANES)
-    back_0, back_1, back_2 = (value.reshape(shape) for value in (back_0, back_1, back_2))
+        )(table, *values, *values, pos, frc, *before)
+
+    near, far = range(2), range(2, n_pairs)
+    acc, reply_0n, nothing = pairs([(0, got[turn], False) for turn in near], [])
+    ready = got[:2] + [value + nothing[None] for value in got[2:]]
+    out = {
+        (kind, group): beyond(jnp.stack([ready[turn][kind] for turn in group]), kind)
+        for group in (near, far)
+        for kind in (1, 2)
+    }
+    acc, reply_1n = pairs([(1, out[1, near], True)], [acc])
+    acc, reply_m = pairs([(0, got[turn], False) for turn in far] + [(2, out[2, near], True)], [acc])
+    acc, reply_f = pairs([(1, out[1, far], True), (2, out[2, far], True)], [acc])
+    reply_0n, reply_1n, reply_m, reply_f = (
+        value.reshape(-1, rows_out, LANES) for value in (reply_0n, reply_1n, reply_m, reply_f)
+    )
+    cut = n_pairs - 2
+    back_0 = jnp.concatenate([reply_0n, reply_m[:cut]])
+    back_1 = beyond(jnp.concatenate([reply_1n, reply_f[:cut]]), 1)
+    back_2 = beyond(jnp.concatenate([reply_m[cut:], reply_f[cut:]]), 2)
     back = []
     for turn in range(n_pairs):
         value = jnp.stack([back_0[turn], back_1[turn], back_2[turn]])

time: 63 us -> 59.3 us (0.941); the launches traced: 63.7 us -> 58.1 us
  waiting for transfers between devices: 14.3 us -> 9.99 us
  starting transfers between devices: 20.6 us -> 17.2 us
  Pallas kernels: 26.4 us -> 28.1 us
    ppermute x4 -> x6, starting transfers between devices: 15.6 us -> 10.4 us  [beyond(): return lax.ppermute(value, 'space', moves)]
    ppermute x6, waiting for transfers between devices: 8.95 us -> 4.09 us  [across(): return lax.ppermute(value, 'pairs', [(j, j ^ turn) for j in range(n_pairs)])]
    pallas_call x4, Pallas kernels: 21 us -> 22.8 us  [pairs(): pl.pallas_call(functools.partial(pair_kernel, sizes, kinds, len(before) =...]
    ppermute x6, starting transfers between devices: 5.06 us -> 6.76 us  [across(): return lax.ppermute(value, 'pairs', [(j, j ^ turn) for j in range(n_pairs)])]
    ppermute x4 -> x6, waiting for transfers between devices: 5.37 us -> 5.9 us  [beyond(): return lax.ppermute(value, 'space', moves)]
  transfers between devices with their start and end apart: 10 -> 12, of which waited for: 6 -> 4; matrix products, arithmetic and copies ran while one was open for 1% -> 2% of each run, Pallas kernels for 21% -> 32%
where the time goes in v1:
time: 59.3 us; the launch traced here: 58.1 us
  Pallas kernels  28.1 us (47%)
  starting transfers between devices  17.2 us (29%)
  waiting for transfers between devices  9.99 us (17%)
  local copies, waits for them, and re-layouts  1.91 us (3%)
  between operations  0.84 us (1%)
    pallas_call x4, Pallas kernels, pairs(): pl.pallas_call(functools.partial(pair_kernel, sizes, kinds, len(before) =...  22.8 us
    ppermute x6, starting transfers between devices, beyond(): return lax.ppermute(value, 'space', moves)  10.4 us
    ppermute x6, starting transfers between devices, across(): return lax.ppermute(value, 'pairs', [(j, j ^ turn) for j in range(n_pairs)])  6.76 us
    ppermute x6, waiting for transfers between devices, beyond(): return lax.ppermute(value, 'space', moves)  5.9 us
    ppermute x6, waiting for transfers between devices, across(): return lax.ppermute(value, 'pairs', [(j, j ^ turn) for j in range(n_pairs)])  4.09 us
    pallas_call x1, Pallas kernels, body(): pl.pallas_call(functools.partial(pack_kernel, sizes), out_shape=[message]...  3.55 us
    pallas_call x1, Pallas kernels, body(): pl.pallas_call(functools.partial(add_kernel, sizes), out_shape=total, in_...  1.72 us
  transfers between devices with their start and end apart: 12, of which 4 were waited for; matrix products, arithmetic and copies ran while one was open for 2% of the time, Pallas kernels for 32%

profile of v1, /device:TPU:0, one launch (start us, length us, event | category | flops | bytes accessed | tf_op | source)
XLA Modules:
  0.0 58.1 jit_solution(120262520823012294)
XLA Ops:
  0.7 3.5 %pack.1 = (f32[3,104,128]{2,1,0:T(8,128)}, f32[3,104,128]{2,1,0:T(8,128)}, f32[3,104,128]{2,1,0:T(8,128)}, f32[3,104,128]{2,1,0:T(8,128)}, s32[49]{0:T(128)}) custom-call(s32[2,48]{1,0:T(2,128)} %cells.1, s32[1]{0:T(128)S(6)} %copy.5.count, f32[768,128]{1,0:T(8,128)} %bitcast.34, f32[768,128]{1,0:T(8,128)} %bitcast.39), custom_call_target="tpu_custom_call" | custom-call | tf_op jit(solution)/shard_map/pack/pallas_call | solution.py:311
  4.2 0.5 collective-permute-start.1
  4.7 2.6 %collective-permute-start = (f32[3,104,128]{2,1,0:T(8,128)}, f32[3,104,128]{2,1,0:T(8,128)S(1)}, u32[]{:S(2)}, u32[]{:S(2)}) collective-permute-start(f32[3,104,128]{2,1,0:T(8,128)} %get-tuple-element.20), channel_id=1, source_target_pairs={{0,2},{1,3},{2,0},{3,1},{4,6},{5,7},{6,4},{7,5},{8,10},{9,11},{10,... | collective-permute-start | bytes 479240 | tf_op jit(solution)/shard_map/ppermute | solution.py:305
  7.3 0.1 collective-permute-start.2
  7.4 0.9 %fusion = (f32[1,104,128]{2,1,0:T(8,128)S(1)}, f32[1,104,128]{2,1,0:T(8,128)S(1)}) fusion(f32[3,104,128]{2,1,0:T(8,128)} %get-tuple-element.21.refs_0_.refs_2_), kind=kLoop, calls=%fused_computation.16 | loop fusion | bytes 212992 | tf_op jit(solution)/shard_map/slice | solution.py:373
  8.3 0.0 collective-permute-done.1.refs_1_.refs_3_
  8.3 1.8 %collective-permute-start.6 = (f32[2,104,128]{2,1,0:T(8,128)S(1)}, f32[2,104,128]{2,1,0:T(8,128)S(1)}, u32[]{:S(2)}, u32[]{:S(2)}) collective-permute-start(f32[2,104,128]{2,1,0:T(8,128)S(1)} %pad_maximum_fusion.3), channel_id=1, source_target_pairs={{0,4},{4,0},{8,12},{12,8},{16,20},{20,16},{24,28},{28,24},{1,5},{5... | collective-permute-start | bytes 319496 | tf_op jit(solution)/shard_map/ppermute | solution.py:309
  10.2 3.6 %collective-permute-start.5 = (f32[2,104,128]{2,1,0:T(8,128)S(1)}, f32[2,104,128]{2,1,0:T(8,128)S(1)}, u32[]{:S(2)}, u32[]{:S(2)}) collective-permute-start(f32[2,104,128]{2,1,0:T(8,128)S(1)} %pad_maximum_fusion.2), channel_id=1, source_target_pairs={{0,28},{4,8},{8,4},{12,16},{16,12},{20,24},{24,20},{28,0},{1,29},{... | collective-permute-start | bytes 319496 | tf_op jit(solution)/shard_map/ppermute | solution.py:309
  13.8 0.9 %copy-done.2 = f32[3,104,128]{2,1,0:T(8,128)S(1)} copy-done((f32[3,104,128]{2,1,0:T(8,128)S(1)}, f32[3,104,128]{2,1,0:T(8,128)}, u32[]{:S(2)}) %copy-start.2) | copy-done | bytes 159768
  14.7 3.9 %pairs.4 = (f32[768,128]{1,0:T(8,128)S(1)}, f32[96,128]{1,0:T(8,128)S(1)}, f32[1,128]{1,0:T(1,128)S(1)}) custom-call(s32[49]{0:T(128)S(1)} %copy-done.3, f32[3,104,128]{2,1,0:T(8,128)S(1)} %copy-done.2, f32[3,104,128]{2,1,0:T(8,128)S(1)} %collective-permute-done.1.refs_1_.refs_3_, f32[3,104,128]{2,1,0:T(8,128)S(1)} %copy-done.2, ...), custom_call_target="tpu_custom_call" | custom-call | flops 2000000000 | bytes 2000000 | tf_op jit(solution)/shard_map/pairs/pallas_call | solution.py:350
  18.6 0.0 collective-permute-done.refs_0_.refs_3_
  18.7 0.0 collective-permute-done.2.refs_1_.refs_4_
  18.7 2.1 %collective-permute-start.4 = (f32[2,104,128]{2,1,0:T(8,128)S(1)}, f32[2,104,128]{2,1,0:T(8,128)S(1)}, u32[]{:S(2)}, u32[]{:S(2)}) collective-permute-start(f32[2,104,128]{2,1,0:T(8,128)S(1)} %pad_maximum_fusion.1), channel_id=1, source_target_pairs={{0,28},{4,8},{8,4},{12,16},{16,12},{20,24},{24,20},{28,0},{1,29},{... | collective-permute-start | bytes 319496 | tf_op jit(solution)/shard_map/ppermute | solution.py:309
  20.9 0.1 collective-permute-start.3
  21.0 0.0 collective-permute-done.6.refs_0_.refs_1_
  21.0 4.8 %pairs.5 = (f32[768,128]{1,0:T(8,128)S(1)}, f32[96,128]{1,0:T(8,128)S(1)}) custom-call(s32[49]{0:T(128)S(1)} %copy-done.3, f32[2,104,128]{2,1,0:T(8,128)S(1)} %collective-permute-done.6.refs_0_.refs_1_, f32[2,104,128]{2,1,0:T(8,128)S(1)} %collective-permute-done.6.refs_0_.refs_1_, f32[768,128]{1,0:T(8,128)S(1)} %bitcast.36, f32[768,128]{1,0:T(8,128)S(1)} %bitcast.41, ...), custom_call_target="tpu_custom_call" | custom-call | flops 2000000000 | bytes 2000000 | tf_op jit(solution)/shard_map/pairs/pallas_call | solution.py:350
  25.8 0.0 collective-permute-done.5.refs_2_.refs_5_
  25.9 9.9 %pairs.6 = (f32[768,128]{1,0:T(8,128)S(1)}, f32[192,128]{1,0:T(8,128)S(1)}) custom-call(s32[49]{0:T(128)S(1)} %copy-done.3, f32[3,104,128]{2,1,0:T(8,128)S(1)} %collective-permute-done.refs_0_.refs_3_, f32[3,104,128]{2,1,0:T(8,128)S(1)} %collective-permute-done.2.refs_1_.refs_4_, f32[2,104,128]{2,1,0:T(8,128)S(1)} %collective-permute-done.5.refs_2_.refs_5_, ...), custom_call_target="tpu_custom_call" | custom-call | flops 4000000000 | bytes 2000000 | tf_op jit(solution)/shard_map/pairs/pallas_call | solution.py:350
  35.8 0.0 collective-permute-done.4.refs_1_.refs_3_
  35.8 0.0 collective-permute-done.3.refs_0_.refs_2_
  35.8 4.2 %pairs.7 = (f32[768,128]{1,0:T(8,128)S(1)}, f32[192,128]{1,0:T(8,128)S(1)}) custom-call(s32[49]{0:T(128)S(1)} %copy-done.3, f32[2,104,128]{2,1,0:T(8,128)S(1)} %collective-permute-done.3.refs_0_.refs_2_, f32[2,104,128]{2,1,0:T(8,128)S(1)} %collective-permute-done.4.refs_1_.refs_3_, f32[2,104,128]{2,1,0:T(8,128)S(1)} %collective-permute-done.3.refs_0_.refs_2_, ...), custom_call_target="tpu_custom_call" | custom-call | flops 4000000000 | bytes 2000000 | tf_op jit(solution)/shard_map/pairs/pallas_call | solution.py:350
  40.0 1.3 %collective-permute-start.7 = (f32[4,48,128]{2,1,0:T(8,128)S(1)}, f32[4,48,128]{2,1,0:T(8,128)S(1)}, u32[]{:S(2)}, u32[]{:S(2)}) collective-permute-start(f32[4,48,128]{2,1,0:T(8,128)S(1)} %pad_maximum_fusion.4), channel_id=1, source_target_pairs={{0,4},{4,0},{8,12},{12,8},{16,20},{20,16},{24,28},{28,24},{1,5},{5... | collective-permute-start | bytes 294920 | tf_op jit(solution)/shard_map/ppermute | solution.py:309
  41.3 1.5 %collective-permute-start.8 = (f32[4,48,128]{2,1,0:T(8,128)S(1)}, f32[4,48,128]{2,1,0:T(8,128)S(1)}, u32[]{:S(2)}, u32[]{:S(2)}) collective-permute-start(f32[4,48,128]{2,1,0:T(8,128)S(1)} %pad_maximum_fusion.5), channel_id=1, source_target_pairs={{0,28},{4,8},{8,4},{12,16},{16,12},{20,24},{24,20},{28,0},{1,29},{... | collective-permute-start | bytes 294920 | tf_op jit(solution)/shard_map/ppermute | solution.py:309
  42.8 1.9 %collective-permute-done.7 = f32[4,48,128]{2,1,0:T(8,128)S(1)} collective-permute-done((f32[4,48,128]{2,1,0:T(8,128)S(1)}, f32[4,48,128]{2,1,0:T(8,128)S(1)}, u32[]{:S(2)}, u32[]{:S(2)}) %collective-permute-start.7) | collective-permute-done | bytes 98336 | tf_op jit(solution)/shard_map/ppermute | solution.py:309
  44.7 4.0 %collective-permute-done.8 = f32[4,48,128]{2,1,0:T(8,128)S(1)} collective-permute-done((f32[4,48,128]{2,1,0:T(8,128)S(1)}, f32[4,48,128]{2,1,0:T(8,128)S(1)}, u32[]{:S(2)}, u32[]{:S(2)}) %collective-permute-start.8) | collective-permute-done | bytes 98336 | tf_op jit(solution)/shard_map/ppermute | solution.py:309
  48.7 3.3 %collective-permute-start.11 = (f32[3,48,128]{2,1,0:T(8,128)S(1)}, f32[3,48,128]{2,1,0:T(8,128)S(1)}, u32[]{:S(2)}, u32[]{:S(2)}) collective-permute-start(f32[3,48,128]{2,1,0:T(8,128)S(1)} %pad_maximum_fusion.9), channel_id=1, source_target_pairs={{0,3},{1,2},{2,1},{3,0},{4,7},{5,6},{6,5},{7,4},{8,11},{9,10},{10,... | collective-permute-start | bytes 221192 | tf_op jit(solution)/shard_map/ppermute | solution.py:305
  52.0 0.2 collective-permute-start.10
  52.2 0.1 collective-permute-start.9
  52.3 2.2 %collective-permute-done.11.refs_3_ = f32[3,48,128]{2,1,0:T(8,128)S(1)} collective-permute-done((f32[3,48,128]{2,1,0:T(8,128)S(1)}, f32[3,48,128]{2,1,0:T(8,128)S(1)}, u32[]{:S(2)}, u32[]{:S(2)}) %collective-permute-start.11) | collective-permute-done | bytes 73760 | tf_op jit(solution)/shard_map/ppermute | solution.py:305
  54.6 1.9 %collective-permute-done.10.refs_2_ = f32[3,48,128]{2,1,0:T(8,128)S(1)} collective-permute-done((f32[3,48,128]{2,1,0:T(8,128)S(1)}, f32[3,48,128]{2,1,0:T(8,128)S(1)}, u32[]{:S(2)}, u32[]{:S(2)}) %collective-permute-start.10) | collective-permute-done | bytes 73760 | tf_op jit(solution)/shard_map/ppermute | solution.py:305
  56.4 0.0 collective-permute-done.9.refs_1_
  56.4 1.7 %add.25 = f32[768,128]{1,0:T(8,128)} custom-call(s32[49]{0:T(128)S(1)} %copy-done.3, f32[768,128]{1,0:T(8,128)S(1)} %get-tuple-element.28.acc, f32[3,48,128]{2,1,0:T(8,128)S(1)} %pad_maximum_fusion.6.refs_0_, f32[3,48,128]{2,1,0:T(8,128)S(1)} %collective-permute-done.9.refs_1_, f32[3,48,128]{2,1,0:T(8,128)S(1)} %collective-permute-done.10.refs_2_, ...), custom_call_target="tpu_custom_call" | custom-call | tf_op jit(solution)/shard_map/add/pallas_call | solution.py:391
  (26 shorter events, 0.2 us)
Async XLA Ops:
  4.2 4.1 %collective-permute-start.1 = (f32[3,104,128]{2,1,0:T(8,128)}, f32[3,104,128]{2,1,0:T(8,128)S(1)}, u32[]{:S(2)}, u32[]{:S(2)}) collective-permute-start(f32[3,104,128]{2,1,0:T(8,128)} %get-tuple-element.22), channel_id=1, source_target_pairs={{0,1},{1,0},{2,3},{3,2},{4,5},{5,4},{6,7},{7,6},{8,9},{9,8},{10,11... | collective-permute-start | bytes 479240 | tf_op jit(solution)/shard_map/ppermute | solution.py:305
  4.7 13.9 %collective-permute-start = (f32[3,104,128]{2,1,0:T(8,128)}, f32[3,104,128]{2,1,0:T(8,128)S(1)}, u32[]{:S(2)}, u32[]{:S(2)}) collective-permute-start(f32[3,104,128]{2,1,0:T(8,128)} %get-tuple-element.20), channel_id=1, source_target_pairs={{0,2},{1,3},{2,0},{3,1},{4,6},{5,7},{6,4},{7,5},{8,10},{9,11},{10,... | collective-permute-start | bytes 479240 | tf_op jit(solution)/shard_map/ppermute | solution.py:305
  7.3 11.4 %collective-permute-start.2 = (f32[3,104,128]{2,1,0:T(8,128)}, f32[3,104,128]{2,1,0:T(8,128)S(1)}, u32[]{:S(2)}, u32[]{:S(2)}) collective-permute-start(f32[3,104,128]{2,1,0:T(8,128)} %get-tuple-element.24), channel_id=1, source_target_pairs={{0,3},{1,2},{2,1},{3,0},{4,7},{5,6},{6,5},{7,4},{8,11},{9,10},{10,... | collective-permute-start | bytes 479240 | tf_op jit(solution)/shard_map/ppermute | solution.py:305
  7.4 6.4 %copy-start = (f32[64,3,512]{2,0,1:T(8,128)S(1)}, f32[64,3,512]{2,0,1:T(8,128)}, u32[]{:S(2)}) copy-start(f32[64,3,512]{2,0,1:T(8,128)} %param.4) | copy-start | bytes 1179652
  7.4 6.4 %copy-start.1 = (f32[64,3,512]{2,0,1:T(8,128)S(1)}, f32[64,3,512]{2,0,1:T(8,128)}, u32[]{:S(2)}) copy-start(f32[64,3,512]{2,0,1:T(8,128)} %param.5) | copy-start | bytes 1179652
  8.3 12.7 %collective-permute-start.6 = (f32[2,104,128]{2,1,0:T(8,128)S(1)}, f32[2,104,128]{2,1,0:T(8,128)S(1)}, u32[]{:S(2)}, u32[]{:S(2)}) collective-permute-start(f32[2,104,128]{2,1,0:T(8,128)S(1)} %pad_maximum_fusion.3), channel_id=1, source_target_pairs={{0,4},{4,0},{8,12},{12,8},{16,20},{20,16},{24,28},{28,24},{1,5},{5... | collective-permute-start | bytes 319496 | tf_op jit(solution)/shard_map/ppermute | solution.py:309
  10.2 3.6 %copy-start.3 = (s32[49]{0:T(128)S(1)}, s32[49]{0:T(128)}, u32[]{:S(2)}) copy-start(s32[49]{0:T(128)} %get-tuple-element.19.table) | copy-start | bytes 592
  10.2 15.7 %collective-permute-start.5 = (f32[2,104,128]{2,1,0:T(8,128)S(1)}, f32[2,104,128]{2,1,0:T(8,128)S(1)}, u32[]{:S(2)}, u32[]{:S(2)}) collective-permute-start(f32[2,104,128]{2,1,0:T(8,128)S(1)} %pad_maximum_fusion.2), channel_id=1, source_target_pairs={{0,28},{4,8},{8,4},{12,16},{16,12},{20,24},{24,20},{28,0},{1,29},{... | collective-permute-start | bytes 319496 | tf_op jit(solution)/shard_map/ppermute | solution.py:309
  13.8 0.9 %copy-start.2 = (f32[3,104,128]{2,1,0:T(8,128)S(1)}, f32[3,104,128]{2,1,0:T(8,128)}, u32[]{:S(2)}) copy-start(f32[3,104,128]{2,1,0:T(8,128)} %get-tuple-element.21.refs_0_.refs_2_) | copy-start | bytes 479236
  18.7 17.0 %collective-permute-start.4 = (f32[2,104,128]{2,1,0:T(8,128)S(1)}, f32[2,104,128]{2,1,0:T(8,128)S(1)}, u32[]{:S(2)}, u32[]{:S(2)}) collective-permute-start(f32[2,104,128]{2,1,0:T(8,128)S(1)} %pad_maximum_fusion.1), channel_id=1, source_target_pairs={{0,28},{4,8},{8,4},{12,16},{16,12},{20,24},{24,20},{28,0},{1,29},{... | collective-permute-start | bytes 319496 | tf_op jit(solution)/shard_map/ppermute | solution.py:309
  20.9 14.9 %collective-permute-start.3 = (f32[2,104,128]{2,1,0:T(8,128)S(1)}, f32[2,104,128]{2,1,0:T(8,128)S(1)}, u32[]{:S(2)}, u32[]{:S(2)}) collective-permute-start(f32[2,104,128]{2,1,0:T(8,128)S(1)} %pad_maximum_fusion), channel_id=1, source_target_pairs={{0,4},{4,0},{8,12},{12,8},{16,20},{20,16},{24,28},{28,24},{1,5},{5... | collective-permute-start | bytes 319496 | tf_op jit(solution)/shard_map/ppermute | solution.py:309
  40.0 4.7 %collective-permute-start.7 = (f32[4,48,128]{2,1,0:T(8,128)S(1)}, f32[4,48,128]{2,1,0:T(8,128)S(1)}, u32[]{:S(2)}, u32[]{:S(2)}) collective-permute-start(f32[4,48,128]{2,1,0:T(8,128)S(1)} %pad_maximum_fusion.4), channel_id=1, source_target_pairs={{0,4},{4,0},{8,12},{12,8},{16,20},{20,16},{24,28},{28,24},{1,5},{5... | collective-permute-start | bytes 294920 | tf_op jit(solution)/shard_map/ppermute | solution.py:309
  41.3 7.4 %collective-permute-start.8 = (f32[4,48,128]{2,1,0:T(8,128)S(1)}, f32[4,48,128]{2,1,0:T(8,128)S(1)}, u32[]{:S(2)}, u32[]{:S(2)}) collective-permute-start(f32[4,48,128]{2,1,0:T(8,128)S(1)} %pad_maximum_fusion.5), channel_id=1, source_target_pairs={{0,28},{4,8},{8,4},{12,16},{16,12},{20,24},{24,20},{28,0},{1,29},{... | collective-permute-start | bytes 294920 | tf_op jit(solution)/shard_map/ppermute | solution.py:309
  48.7 5.8 %collective-permute-start.11 = (f32[3,48,128]{2,1,0:T(8,128)S(1)}, f32[3,48,128]{2,1,0:T(8,128)S(1)}, u32[]{:S(2)}, u32[]{:S(2)}) collective-permute-start(f32[3,48,128]{2,1,0:T(8,128)S(1)} %pad_maximum_fusion.9), channel_id=1, source_target_pairs={{0,3},{1,2},{2,1},{3,0},{4,7},{5,6},{6,5},{7,4},{8,11},{9,10},{10,... | collective-permute-start | bytes 221192 | tf_op jit(solution)/shard_map/ppermute | solution.py:305
  52.0 4.4 %collective-permute-start.10 = (f32[3,48,128]{2,1,0:T(8,128)S(1)}, f32[3,48,128]{2,1,0:T(8,128)S(1)}, u32[]{:S(2)}, u32[]{:S(2)}) collective-permute-start(f32[3,48,128]{2,1,0:T(8,128)S(1)} %pad_maximum_fusion.8), channel_id=1, source_target_pairs={{0,2},{1,3},{2,0},{3,1},{4,6},{5,7},{6,4},{7,5},{8,10},{9,11},{10,... | collective-permute-start | bytes 221192 | tf_op jit(solution)/shard_map/ppermute | solution.py:305
  52.2 4.2 %collective-permute-start.9 = (f32[3,48,128]{2,1,0:T(8,128)S(1)}, f32[3,48,128]{2,1,0:T(8,128)S(1)}, u32[]{:S(2)}, u32[]{:S(2)}) collective-permute-start(f32[3,48,128]{2,1,0:T(8,128)S(1)} %pad_maximum_fusion.7), channel_id=1, source_target_pairs={{0,1},{1,0},{2,3},{3,2},{4,5},{5,4},{6,7},{7,6},{8,9},{9,8},{10,11... | collective-permute-start | bytes 221192 | tf_op jit(solution)/shard_map/ppermute | solution.py:305
